TPU v7x, 32 devices: a whole 2x2x4 slice. The times are simulated.
32 devices in a mesh: kmer: 8 (over z, y), samp: 4 (over x, core).
Axes of the slice: x: 2, y: 2, z: 4, core: 2. Of those that a mesh axis runs over, the one named last changes fastest.
Arguments:
- abundance: float32 [16384, 4096], P('kmer', 'samp'), may hold values from 1 to 100
- loadings: float32 [16384, 256], P('kmer', 'samp'), may hold values from 0.01 to 5, as said below
- activity: float32 [256, 4096], P('kmer', 'samp'), may hold values from 0.01 to 5, as said below
Outputs:
- new_loadings: float32 [16384, 256], P('kmer', 'samp')
- new_activity: float32 [256, 4096], P('kmer', 'samp')
Inputs may be any that keep to these rules, and one draw needn't show every extreme that they name: `loadings`: positive entries. `activity`: positive entries.
All inputs are finite; a program needn't handle non-finite values.
Results may differ from a plain program's by a relative error of at most 0.0001.
Values sent between devices are 32-bit elements; how exact they have to be, the bound alone decides.
A program may use at most 64 MiB of HBM per device.

v0:
```python
import jax
import jax.numpy as jnp
from jax import lax
from jax.sharding import PartitionSpec as P


def per_device(abundance, loadings, activity):
    highest = lax.Precision.HIGHEST
    rank = activity.shape[0] * lax.axis_size("kmer")
    samp_width = rank // lax.axis_size("samp")
    kmer_width = rank // lax.axis_size("kmer")
    activity_all = lax.all_gather(activity, "kmer", axis=0, tiled=True)
    loadings_all = lax.all_gather(loadings, "samp", axis=1, tiled=True)
    row_totals = jnp.sum(activity_all, axis=1)
    rebuilt = jnp.dot(
        loadings_all, activity_all, precision=highest, preferred_element_type=jnp.float32
    )
    quotient = abundance / rebuilt
    numer_terms = lax.dot_general(
        quotient,
        activity_all,
        (((1,), (1,)), ((), ())),
        precision=highest,
        preferred_element_type=jnp.float32,
    )
    numer_whole, totals_whole = lax.psum((numer_terms, row_totals), "samp")
    updated_all = loadings_all * numer_whole / totals_whole
    new_loadings = lax.dynamic_slice_in_dim(
        updated_all, lax.axis_index("samp") * samp_width, samp_width, 1
    )
    column_terms = jnp.sum(updated_all, axis=0)
    rebuilt_again = jnp.dot(
        updated_all, activity_all, precision=highest, preferred_element_type=jnp.float32
    )
    quotient_again = abundance / rebuilt_again
    numer_h_terms = lax.dot_general(
        updated_all,
        quotient_again,
        (((0,), (0,)), ((), ())),
        precision=highest,
        preferred_element_type=jnp.float32,
    )
    numer_h = lax.psum_scatter(numer_h_terms, "kmer", scatter_dimension=0, tiled=True)
    column_sums = lax.psum(column_terms, "kmer")
    sums_share = lax.dynamic_slice_in_dim(
        column_sums, lax.axis_index("kmer") * kmer_width, kmer_width, 0
    )[:, None]
    new_activity = activity * numer_h / sums_share
    return (new_loadings, new_activity)


def solution(mesh):
    in_specs = (P("kmer", "samp"), P("kmer", "samp"), P("kmer", "samp"))
    out_specs = (P("kmer", "samp"), P("kmer", "samp"))
    return jax.shard_map(
        per_device, mesh=mesh, in_specs=in_specs, out_specs=out_specs, check_vma=False
    )
```

profile of v0, /device:TPU:0, one launch (start us, length us, event | category | flops | bytes accessed | tf_op | source)
XLA Modules:
  0.0 238.2 jit_solution(6746515739964624756)
XLA Ops:
  7.2 0.0 all-gather.5.cloned.1.call-start
  7.2 0.7 all-gather.5.cloned.1.call-update
  7.9 0.0 all-gather.3.cloned.1.call-start
  7.9 0.7 all-gather.3.cloned.1.call-update
  8.6 0.0 all-reduce.2.cloned.1.call-start
  8.7 44.3 %all-gather.5.cloned.1.call-done = f32[256,1024]{1,0:T(8,128)} async-done(((f32[32,1024]{1,0:T(8,128)}), f32[256,1024]{1,0:T(8,128)}) %all-gather.5.cloned.1.call-update) | async-done | bytes 1048592 | tf_op jit(solution)/shard_map/all_gather | solution.py:12
  53.0 22.9 %all-gather.3.cloned.1.call-done = f32[2048,256]{0,1:T(8,128)} async-done(((f32[2048,64]{0,1:T(8,128)}), f32[2048,256]{0,1:T(8,128)}) %all-gather.3.cloned.1.call-update) | async-done | bytes 2097168 | tf_op jit(solution)/shard_map/all_gather | solution.py:13
  75.9 9.3 %fusion.5 = f32[2048,1024]{1,0:T(8,128)S(1)} fusion(f32[2048,256]{0,1:T(8,128)} %all-gather.3.cloned.1.call-done, f32[256,1024]{1,0:T(8,128)} %all-gather.5.cloned.1.call-done), kind=kOutput, calls=%fused_computation.8 | convolution fusion | flops 6442450944 | bytes 11534336 | tf_op jit(solution)/shard_map/dot_general | solution.py:15
  85.2 0.0 copy-done.1
  85.2 10.2 %fusion.2 = f32[2048,256]{1,0:T(8,128)} fusion(f32[256,1024]{1,0:T(8,128)S(1)} %copy-done.1, f32[2048,1024]{1,0:T(8,128)} %param.3, f32[2048,1024]{1,0:T(8,128)S(1)} %fusion.5), kind=kOutput, calls=%fused_computation.2 | convolution fusion | flops 6444548096 | bytes 19922944 | tf_op jit(solution)/shard_map/dot_general | solution.py:19
  95.4 0.0 all-reduce.2.cloned.1.call-update
  95.5 0.0 reduce-scatter.2.cloned.1.call-start
  95.5 0.1 reduce_sum.18
  95.7 6.0 %psum.22 = f32[256]{0:T(256)S(1)} all-reduce(f32[256]{0:T(256)S(1)} %reduce_sum.18), channel_id=1, replica_groups=mesh['kmer'=8,'samp'=4] {'samp'}, use_global_device_ids=true, to_apply=%region_2.0 | all-reduce | flops 256 | bytes 2048 | tf_op jit(solution)/shard_map/psum | solution.py:26
  101.7 0.0 copy-done
  101.7 1.9 copy.7
  103.5 43.5 %all-reduce.2.cloned.1.call-done = f32[2048,256]{1,0:T(8,128)} async-done(((f32[2048,256]{1,0:T(8,128)}), f32[2048,256]{1,0:T(8,128)}) %all-reduce.2.cloned.1.call-update) | async-done | bytes 2097168 | tf_op jit(solution)/shard_map/psum | solution.py:26
  147.0 2.7 %fusion.4 = (f32[256]{0:T(256)S(1)}, f32[2048,256]{1,0:T(8,128)S(1)}) fusion(f32[256]{0:T(256)S(1)} %psum.22, f32[2048,256]{1,0:T(8,128)} %copy.7, f32[2048,256]{1,0:T(8,128)} %all-reduce.2.cloned.1.call-done), kind=kLoop, calls=%fused_computation.7 | loop fusion | flops 1572608 | bytes 6293504 | tf_op jit(solution)/shard_map/reduce_sum | solution.py:31
  149.7 0.0 slice-start.1
  149.8 7.7 %fusion.6 = f32[2048,1024]{1,0:T(8,128)S(1)} fusion(f32[2048,256]{1,0:T(8,128)S(1)} %get-tuple-element.7, f32[256,1024]{1,0:T(8,128)S(1)} %copy-done.1), kind=kOutput, calls=%fused_computation.9 | convolution fusion | flops 6442450944 | bytes 11534336 | tf_op jit(solution)/shard_map/dot_general | solution.py:32
  157.4 0.0 slice-done
  157.5 0.0 slice-done.1
  157.5 8.8 %fusion = f32[256,1024]{1,0:T(8,128)} fusion(f32[2048,256]{1,0:T(8,128)S(1)} %get-tuple-element.7, f32[2048,1024]{1,0:T(8,128)S(1)} %bitcast.7, f32[2048,1024]{1,0:T(8,128)S(1)} %fusion.6), kind=kOutput, calls=%fused_computation | convolution fusion | flops 6444548096 | bytes 19922944 | tf_op jit(solution)/shard_map/dot_general | solution.py:36
  166.3 0.0 reduce-scatter.2.cloned.1.call-update
  166.3 0.0 copy-start.2
  166.3 0.3 constant_dynamic-slice_fusion
  166.7 1.1 copy.8
  167.8 21.6 %psum.23 = f32[256]{0:T(256)S(1)} all-reduce(f32[256]{0:T(256)S(1)} %get-tuple-element.6), channel_id=1, replica_groups=mesh['kmer'=8,'samp'=4] {'kmer'}, use_global_device_ids=true, to_apply=%region_5.0 | all-reduce | flops 256 | bytes 2048 | tf_op jit(solution)/shard_map/psum | solution.py:44
  189.3 0.1 dynamic_slice.7
  189.4 40.6 %reduce-scatter.2.cloned.1.call-done = f32[32,1024]{1,0:T(8,128)} async-done(((f32[256,1024]{1,0:T(8,128)}), f32[32,1024]{1,0:T(8,128)}) %reduce-scatter.2.cloned.1.call-update) | async-done | bytes 131088 | tf_op jit(solution)/shard_map/reduce_scatter | solution.py:43
  230.0 0.0 copy-done.2
  230.0 1.6 multiply_divide_fusion.1
  (4 shorter events, 0.0 us)
Async XLA Ops:
  7.2 45.8 %all-gather.5.cloned.1.call-start = ((), (), s32[]{:S(2)}) async-start(), calls=%async_computation.2 | async-start | bytes 1179648 | tf_op jit(solution)/shard_map/all_gather | solution.py:12
  7.9 68.0 %all-gather.3.cloned.1.call-start = ((), (), s32[]{:S(2)}) async-start(), calls=%async_computation.1 | async-start | bytes 2621440 | tf_op jit(solution)/shard_map/all_gather | solution.py:13
  8.6 138.4 %all-reduce.2.cloned.1.call-start = ((), (), s32[]{:S(2)}) async-start(), calls=%async_computation.3 | async-start | bytes 4194304 | tf_op jit(solution)/shard_map/psum | solution.py:26
  53.0 32.2 %copy-start.1 = (f32[256,1024]{1,0:T(8,128)S(1)}, f32[256,1024]{1,0:T(8,128)}, u32[]{:S(2)}) copy-start(f32[256,1024]{1,0:T(8,128)} %all-gather.5.cloned.1.call-done) | copy-start | bytes 3145732
  95.4 6.2 %copy-start = (f32[2048,256]{0,1:T(8,128)S(1)}, f32[2048,256]{0,1:T(8,128)}, u32[]{:S(2)}) copy-start(f32[2048,256]{0,1:T(8,128)} %all-gather.3.cloned.1.call-done) | copy-start | bytes 6291460
  95.5 134.5 %reduce-scatter.2.cloned.1.call-start = ((), (), s32[]{:S(2)}) async-start(), calls=%async_computation.4 | async-start | bytes 1179648 | tf_op jit(solution)/shard_map/reduce_scatter | solution.py:43
  147.0 10.4 %slice-start = ((s8[8388608]{0:T(1024)(128)(4,1)}), s8[4194304]{0:T(1024)(128)(4,1)S(1)}, s32[]{:S(2)}) async-start(s8[8388608]{0:T(1024)(128)(4,1)} %bitcast.6), calls=%async_computation.5 | async-start | bytes 8388608
  149.7 7.7 %slice-start.1 = ((s8[8388608]{0:T(1024)(128)(4,1)}), s8[4194304]{0:T(1024)(128)(4,1)S(1)}, s32[]{:S(2)}) async-start(s8[8388608]{0:T(1024)(128)(4,1)} %bitcast.6), calls=%async_computation.6 | async-start | bytes 8388608
  166.3 63.7 %copy-start.2 = (f32[32,1024]{1,0:T(8,128)S(1)}, f32[32,1024]{1,0:T(8,128)}, u32[]{:S(2)}) copy-start(f32[32,1024]{1,0:T(8,128)} %param.5) | copy-start | bytes 393220
Sparse Core Ops, SparseCore 0:
  10.1 42.8 all-gather.4
  54.6 21.3 all-gather.2
  95.6 51.3 all-reduce.1
  166.4 63.5 reduce-scatter.1
where the time goes:
time: 238 us
  waiting for transfers between devices  153 us (64%)
  matrix products  36 us (15%)
  blocking collectives  27.6 us (12%)
  between operations  13.8 us (6%)
  other arithmetic  4.52 us (2%)
  local copies, waits for them, and re-layouts  3.41 us (1%)
    all_gather x1, waiting for transfers between devices, per_device(): activity_all = lax.all_gather(activity, 'kmer', axis=0, tiled=True)  44.3 us
    psum x1, waiting for transfers between devices, per_device(): numer_whole, totals_whole = lax.psum((numer_terms, row_totals), 'samp')  43.5 us
    reduce_scatter x1, waiting for transfers between devices, per_device(): lax.psum_scatter(numer_h_terms, 'kmer', scatter_dimension=0, tiled=True)  40.6 us
    all_gather x1, waiting for transfers between devices, per_device(): loadings_all = lax.all_gather(loadings, 'samp', axis=1, tiled=True)  22.9 us
    psum x1, blocking collectives, per_device(): column_sums = lax.psum(column_terms, 'kmer')  21.6 us
    dot_general x1, matrix products, per_device(): lax.dot_general(quotient, activity_all, (((1,), (1,)), ((), ())), precisi...  10.2 us
    dot_general x1, matrix products, per_device(): jnp.dot(loadings_all, activity_all, precision=highest, preferred_element_...  9.26 us
    dot_general x1, matrix products, per_device(): lax.dot_general(updated_all, quotient_again, (((0,), (0,)), ((), ())), pr...  8.82 us
  transfers between devices with their start and end apart: 4, of which 4 were waited for; matrix products, arithmetic and copies ran while one was open for 1% of the time, Pallas kernels for 0%

commit v1 on v0

v1 whole, which is shorter than its diff:
```python
import functools

import jax
import jax.numpy as jnp
from jax import lax
from jax.experimental import pallas as pl
from jax.experimental.pallas import tpu as pltpu
from jax.sharding import PartitionSpec as P

F32, BF16 = jnp.float32, jnp.bfloat16
LANES = 128
CORES = 2


def halves(value):
    high = value.astype(BF16)
    return high, (value - high.astype(F32)).astype(BF16)


def quotient_of(above, below):
    guess = pl.reciprocal(below, approx=True)
    return above * (guess * (2.0 - below * guess))


def dot(a, b):
    return jnp.dot(a, b, preferred_element_type=F32)


def kernel(
    sizes, ab_hbm, load_ref, act_ref, newload_ref, newact_ref,
    ab, wbuf, wfull, w3, hbuf, h3, ht3, tbuf, nbuf, recv_a, sbuf, recv_x, ubuf, acc, recv_y, ybuf, recv_z,
    ab_sem, hz_s, hy_s, h_r, wx_s, wc_s, wf_s, w_r, t_s, t_r, a_s, a_r, x_s, x_r, u_s, u_r, ry_s, ry_r, rz_s, rz_r,
):
    n_k, n_s, n_z, n_y, chunk = sizes
    n_x = n_s // CORES
    rows_m, width = load_ref.shape
    rows_h, cols = act_ref.shape
    rank = rows_h * n_k
    per_tile = LANES // width
    packed = rows_m // per_tile
    pieces = packed // chunk
    chunks = rows_m // chunk
    half = chunk // 2

    k, s = lax.axis_index("kmer"), lax.axis_index("samp")
    z, y = lax.div(k, n_y), lax.rem(k, n_y)
    x, core = lax.div(s, CORES), lax.rem(s, CORES)
    mate = x * CORES + (1 - core)

    def z_at(d):
        return lax.rem(z + d, n_z)

    def y_at(d):
        return lax.rem(y + d, n_y)

    def x_at(d):
        return lax.rem(x + d, n_x) * CORES + core

    def put(src, dst, send, recv, kk, ss):
        return pltpu.make_async_remote_copy(
            src_ref=src, dst_ref=dst, send_sem=send, recv_sem=recv,
            device_id={"kmer": kk, "samp": ss}, device_id_type=pl.DeviceIdType.MESH,
        )

    def block(start, size):
        return pl.ds(pl.multiple_of(start, size), size)

    def arrived(dst, sem):
        put(dst, dst, sem, sem, k, mate).wait_recv()

    sent = []

    def go(*args):
        copy = put(*args)
        copy.start()
        sent.append(copy)

    fetch = pltpu.make_async_copy(ab_hbm, ab, ab_sem)
    fetch.start()

    hbuf[block(k * rows_h, rows_h), :] = act_ref[...]
    wbuf[s] = jnp.concatenate([load_ref[q * packed:(q + 1) * packed, :] for q in range(per_tile)], axis=1)

    barrier = pltpu.get_barrier_semaphore()
    peers = [(z_at(d) * n_y + y, s) for d in range(1, n_z)]
    peers += [(z * n_y + y_at(d), s) for d in range(1, n_y)]
    peers += [(k, lax.rem(s + d, n_s)) for d in range(1, n_s)]
    for kk, ss in peers:
        pl.semaphore_signal(
            barrier, inc=1, device_id={"kmer": kk, "samp": ss}, device_id_type=pl.DeviceIdType.MESH
        )
    pl.semaphore_wait(barrier, len(peers))

    near = []
    for d in range(1, n_z // 2 + 1):
        near += [d] if d == n_z - d else [d, n_z - d]

    def hslot(kk):
        return hbuf.at[block(kk * rows_h, rows_h), :]

    def wslot(ss, j):
        return wbuf.at[ss, pl.ds(j * chunk, chunk), :]

    def pass_y(i, zz):
        slot = hslot(zz * n_y + y)
        for d in range(1, n_y):
            go(slot, slot, hy_s.at[i, d - 1], h_r.at[zz * n_y + y], z * n_y + y_at(d), s)

    for i, d in enumerate(near):
        go(hslot(k), hslot(k), hz_s.at[i], h_r.at[k], z_at(d) * n_y + y, s)
        if i == 0:
            pass_y(0, z)
    for j in range(pieces):
        for d in range(1, n_x):
            go(wslot(s, j), wslot(s, j), wx_s.at[d - 1, j], w_r.at[s, j], k, x_at(d))
        go(wslot(s, j), wslot(s, j), wc_s.at[j], w_r.at[s, j], k, mate)

    def take_h(i):
        src = lax.rem(z + n_z - near[i], n_z)
        arrived(hslot(src * n_y + y), h_r.at[src * n_y + y])
        pass_y(i + 1, src)

    def take_w(j):
        for d in range(1, n_x):
            src = x_at(d)
            arrived(wslot(src, j), w_r.at[src, j])
            go(wslot(src, j), wslot(src, j), wf_s.at[d - 1, j], w_r.at[src, j], k, mate)

    for i in range(max(len(near), pieces)):
        if i < len(near):
            take_h(i)
        if i < pieces:
            take_w(i)

    for j in range(pieces):
        for d in range(n_x):
            src = lax.rem(x + d, n_x) * CORES + (1 - core)
            arrived(wslot(src, j), w_r.at[src, j])
        for q in range(per_tile):
            at = q * packed + j * chunk
            whole = jnp.concatenate(
                [wbuf[i, j * chunk:(j + 1) * chunk, q * width:(q + 1) * width] for i in range(n_s)], axis=1
            )
            wfull[at:at + chunk, :] = whole
            high, low = halves(whole)
            w3[at:at + chunk, :] = jnp.concatenate([high, high, low], axis=1)

    for d in range(1, n_y):
        for i in range(n_z):
            src = i * n_y + y_at(d)
            arrived(hslot(src), h_r.at[src])

    high, low = halves(hbuf[...])
    h3[...] = jnp.concatenate([high, low, high], axis=0)
    turned = hbuf[...].T
    high, low = halves(turned)
    ht3[...] = jnp.concatenate([high, low, high], axis=0)
    tbuf[s] = jnp.broadcast_to(jnp.sum(turned, axis=0, keepdims=True), (8, rank))
    for d in range(1, n_s):
        go(tbuf.at[s], tbuf.at[s], t_s.at[d - 1], t_r.at[s], k, lax.rem(s + d, n_s))
    fetch.wait()

    def out_a(c):
        return put(
            nbuf.at[block(c * chunk + (1 - core) * half, half), :], recv_a.at[block(c * half, half), :],
            a_s.at[c], a_r.at[c], k, mate,
        )

    def out_x(c, d):
        rows = block(c * half, half)
        return put(sbuf.at[rows, :], recv_x.at[d - 1, rows, :], x_s.at[d - 1, c], x_r.at[d - 1, c], k, x_at(d))

    def out_u(c):
        rows = block(c * chunk + core * half, half)
        return put(ubuf.at[rows, :], ubuf.at[rows, :], u_s.at[c], u_r.at[c], k, mate)

    def rows_step(c, carry):
        @pl.when(c < chunks)
        def _():
            rows = block(c * chunk, chunk)
            quotient = quotient_of(ab[rows, :], dot(w3[rows, :], h3[...]))
            high, low = halves(quotient)
            nbuf[rows, :] = dot(jnp.concatenate([high, high, low], axis=1), ht3[...])
            out_a(c).start()

        @pl.when(c >= 1)
        def _():
            b = c - 1
            out_a(b).wait_recv()
            rows = block(b * half, half)
            sbuf[rows, :] = nbuf[block(b * chunk + core * half, half), :] + recv_a[rows, :]
            for d in range(1, n_x):
                out_x(b, d).start()

        return carry

    lax.fori_loop(0, chunks + 1, rows_step, 0)

    for d in range(1, n_s):
        src = lax.rem(s + d, n_s)
        arrived(tbuf.at[src], t_r.at[src])
    totals = tbuf[0, 0:1, :]
    for i in range(1, n_s):
        totals = totals + tbuf[i, 0:1, :]
    scale = 1.0 / totals
    acc[...] = jnp.zeros_like(acc)

    def cols_step(c, carry):
        @pl.when(c < chunks)
        def _():
            rows = block(c * half, half)
            total = sbuf[rows, :]
            for d in range(1, n_x):
                out_x(c, d).wait_recv()
                total = total + recv_x[d - 1, rows, :]
            mine = block(c * chunk + core * half, half)
            ubuf[mine, :] = wfull[mine, :] * total * scale
            out_u(c).start()

        @pl.when(c >= 1)
        def _():
            b = c - 1
            out_u(b).wait_recv()
            rows = block(b * chunk, chunk)
            updated = ubuf[rows, :]
            high, low = halves(updated)
            rebuilt = dot(jnp.concatenate([high, high, low], axis=1), h3[...])
            q_high, q_low = halves(quotient_of(ab[rows, :], rebuilt))
            turned = updated.T
            high, low = halves(turned)
            acc[:, :cols] += dot(
                jnp.concatenate([high, high, low], axis=1), jnp.concatenate([q_high, q_low, q_high], axis=0)
            )
            acc[:, cols:] += jnp.broadcast_to(jnp.sum(turned, axis=1, keepdims=True), (rank, LANES))

        return carry

    lax.fori_loop(0, chunks + 1, cols_step, 0)

    far = near[::-1] + [0]
    for i, d in enumerate(far):
        for e in range(1, n_y):
            go(
                acc.at[block((z_at(d) * n_y + y_at(e)) * rows_h, rows_h), :], recv_y.at[e - 1, i],
                ry_s.at[e - 1, i], ry_r.at[e - 1, i], z * n_y + y_at(e), s,
            )

    for i in range(n_s):
        @pl.when(s == i)
        def _():
            newload_ref[...] = ubuf[:, i * width:(i + 1) * width]

    total = None
    for i, d in enumerate(far):
        total = acc[block((z_at(d) * n_y + y) * rows_h, rows_h), :]
        for e in range(1, n_y):
            arrived(recv_y.at[e - 1, i], ry_r.at[e - 1, i])
            total = total + recv_y[e - 1, i]
        if d:
            ybuf[i] = total
            go(ybuf.at[i], recv_z.at[i], rz_s.at[i], rz_r.at[i], z_at(d) * n_y + y, s)
    for i in range(n_z - 1):
        arrived(recv_z.at[i], rz_r.at[i])
        total = total + recv_z[i]
    newact_ref[...] = act_ref[...] * total[:, :cols] / total[:, cols:cols + 1]

    for copy in sent:
        copy.wait_send()

    def close(c, carry):
        out_a(c).wait_send()
        out_u(c).wait_send()
        for d in range(1, n_x):
            out_x(c, d).wait_send()
        return carry

    lax.fori_loop(0, chunks, close, 0)


def solution(mesh):
    n_k, n_s = mesh.shape["kmer"], mesh.shape["samp"]
    n_y = max(d for d in range(1, n_k + 1) if n_k % d == 0 and d * d <= n_k)
    n_z, n_x = n_k // n_y, n_s // CORES

    def per_device(abundance, loadings, activity):
        rows_m, width = loadings.shape
        rows_h, cols = activity.shape
        rank = rows_h * n_k
        packed = rows_m * width // LANES
        chunk = min(256, packed)
        chunks, pieces = rows_m // chunk, packed // chunk
        vmem, dma = pltpu.VMEM, pltpu.SemaphoreType.DMA
        whole = pl.BlockSpec(memory_space=pltpu.VMEM)
        return pl.pallas_call(
            functools.partial(kernel, (n_k, n_s, n_z, n_y, chunk)),
            out_shape=(
                jax.ShapeDtypeStruct((rows_m, width), F32),
                jax.ShapeDtypeStruct((rows_h, cols), F32),
            ),
            in_specs=[pl.BlockSpec(memory_space=pl.ANY), whole, whole],
            out_specs=(whole, whole),
            scratch_shapes=[
                vmem((rows_m, cols), F32),
                vmem((n_s, packed, LANES), F32),
                vmem((rows_m, rank), F32),
                vmem((rows_m, 3 * rank), BF16),
                vmem((rank, cols), F32),
                vmem((3 * rank, cols), BF16),
                vmem((3 * cols, rank), BF16),
                vmem((n_s, 8, rank), F32),
                vmem((rows_m, rank), F32),
                vmem((rows_m // 2, rank), F32),
                vmem((rows_m // 2, rank), F32),
                vmem((n_x - 1, rows_m // 2, rank), F32),
                vmem((rows_m, rank), F32),
                vmem((rank, cols + LANES), F32),
                vmem((n_y - 1, n_z, rows_h, cols + LANES), F32),
                vmem((n_z - 1, rows_h, cols + LANES), F32),
                vmem((n_z - 1, rows_h, cols + LANES), F32),
                dma,
                dma((n_z - 1,)),
                dma((n_z, n_y - 1)),
                dma((n_k,)),
                dma((n_x - 1, pieces)),
                dma((pieces,)),
                dma((n_x - 1, pieces)),
                dma((n_s, pieces)),
                dma((n_s - 1,)),
                dma((n_s,)),
                dma((chunks,)),
                dma((chunks,)),
                dma((n_x - 1, chunks)),
                dma((n_x - 1, chunks)),
                dma((chunks,)),
                dma((chunks,)),
                dma((n_y - 1, n_z)),
                dma((n_y - 1, n_z)),
                dma((n_z - 1,)),
                dma((n_z - 1,)),
            ],
            compiler_params=pltpu.CompilerParams(
                collective_id=0, has_side_effects=True, vmem_limit_bytes=56 * 2**20
            ),
            cost_estimate=pl.CostEstimate(
                flops=24 * rows_m * cols * rank,
                bytes_accessed=4 * rows_m * cols,
                transcendentals=2 * rows_m * cols,
            ),
        )(abundance, loadings, activity)

    in_specs = (P("kmer", "samp"), P("kmer", "samp"), P("kmer", "samp"))
    out_specs = (P("kmer", "samp"), P("kmer", "samp"))
    return jax.shard_map(
        per_device, mesh=mesh, in_specs=in_specs, out_specs=out_specs, check_vma=False
    )
```

time: 238 us -> 81.3 us (0.34)
  waiting for transfers between devices: 153 us -> 0 us
  Pallas kernels: 0 us -> 73.9 us
  matrix products: 36 us -> 0 us
  blocking collectives: 27.6 us -> 0 us
  between operations: 13.8 us -> 0.64 us
  other arithmetic: 4.52 us -> 0 us
  local copies, waits for them, and re-layouts: 3.41 us -> 6.27 us
    pallas_call x0 -> x1, Pallas kernels: none -> 73.9 us  [per_device(): pl.pallas_call(functools.partial(kernel, (n_k, n_s, n_z, n_y, chunk)), ou...]
    all_gather x2 -> x0, waiting for transfers between devices: 67.2 us -> none  [the longest x1 44.3 us: per_device(): activity_all = lax.all_gather(activity, 'kmer', axis=0, tiled=True)]
    psum x1 -> x0, waiting for transfers between devices: 43.5 us -> none  [per_device(): numer_whole, totals_whole = lax.psum((numer_terms, row_totals), 'samp')]
    reduce_scatter x1 -> x0, waiting for transfers between devices: 40.6 us -> none  [per_device(): lax.psum_scatter(numer_h_terms, 'kmer', scatter_dimension=0, tiled=True)]
    dot_general x4 -> x0, matrix products: 36 us -> none  [the longest x1 10.2 us: per_device(): lax.dot_general(quotient, activity_all, (((1,), (1,)), ((), ())), precisi...]
    psum x2 -> x0, blocking collectives: 27.6 us -> none  [the longest x1 21.6 us: per_device(): column_sums = lax.psum(column_terms, 'kmer')]
    reduce_sum x2 -> x0, other arithmetic: 2.88 us -> none  [the longest x1 2.74 us: per_device(): column_terms = jnp.sum(updated_all, axis=0)]
    unnamed x11 -> x2, local copies, waits for them, and re-layouts: 1.13 us -> 3.94 us
  transfers between devices with their start and end apart: 4 -> 0, of which waited for: 4 -> 0; matrix products, arithmetic and copies ran while one was open for 1% -> 0% of each run, Pallas kernels for 0% -> 0%
where the time goes in v1:
time: 81.3 us; the launch traced here: 80.8 us
  Pallas kernels  73.9 us (91%)
  local copies, waits for them, and re-layouts  6.27 us (8%)
    pallas_call x1, Pallas kernels, per_device(): pl.pallas_call(functools.partial(kernel, (n_k, n_s, n_z, n_y, chunk)), ou...  73.9 us
    unnamed x2, local copies, waits for them, and re-layouts  3.94 us
    pallas_call x1, local copies, waits for them, and re-layouts, per_device(): pl.pallas_call(functools.partial(kernel, (n_k, n_s, n_z, n_y, chunk)), ou...  2.34 us

profile of v1, /device:TPU:0, one launch (start us, length us, event | category | flops | bytes accessed | tf_op | source)
XLA Modules:
  0.0 80.8 jit_solution(6715400216105145630)
XLA Ops:
  0.6 2.4 %copy.5.load_ref = f32[2048,64]{1,0:T(8,128)} copy(f32[2048,64]{0,1:T(8,128)} %param.4) | data formatting | bytes 1048576 | tf_op args[1]
  3.0 73.9 %shard_map.50 = (f32[2048,64]{1,0:T(8,128)}, f32[32,1024]{1,0:T(8,128)}) custom-call(f32[2048,1024]{1,0:T(8,128)} %ab_hbm.1, f32[2048,64]{1,0:T(8,128)} %copy.5.load_ref, f32[32,1024]{1,0:T(8,128)} %act_ref.1), custom_call_target="tpu_custom_call" | custom-call | flops 12884901888 | bytes 8388608 | tf_op jit(solution)/shard_map/pallas_call | solution.py:294
  76.9 2.3 %copy.6 = f32[2048,64]{0,1:T(8,128)} copy(f32[2048,64]{1,0:T(8,128)} %get-tuple-element.2) | data formatting | bytes 1048576 | tf_op jit(solution)/shard_map/pallas_call | solution.py:294
  79.2 1.6 %copy.8 = f32[32,1024]{1,0:T(8,128)} copy(f32[32,1024]{1,0:T(8,128)} %get-tuple-element.7) | data formatting | bytes 262144

commit v2 on v1

v2 whole, which is shorter than its diff:
```python
import functools

import jax
import jax.numpy as jnp
from jax import lax
from jax.experimental import pallas as pl
from jax.experimental.pallas import tpu as pltpu
from jax.sharding import PartitionSpec as P

F32, BF16 = jnp.float32, jnp.bfloat16
LANES = 128
PIECE = 512
PARTS = 2
FLYING = 3
CORES = 2


def halves(value):
    high = value.astype(BF16)
    return high, (value - high.astype(F32)).astype(BF16)


def quotient_of(above, below):
    guess = pl.reciprocal(below, approx=True)
    return above * (guess * (2.0 - below * guess))


def dot(a, b):
    return jnp.dot(a, b, preferred_element_type=F32)


def kernel(
    sizes, ab_hbm, load_ref, act_ref, newload_ref, newact_ref,
    ab, wbuf, wfull, w3, hbuf, h3, ht3, tbuf, tsum, nbuf, recv_a, sbuf, recv_x, ubuf, uturn, acc, cbuf, csum, recv_y, ybuf, recv_z,
    ab_sem, hr_s, hl_s, hy_s, h_r, wx_s, wc_s, wf_s, w_r, t_s, t_r, a_s, a_r, x_s, x_r, u_s, u_r, c_s, c_r,
    ry_s, ry_r, rz_s, rz_r,
):
    n_k, n_s, n_z, n_y, chunk = sizes
    n_x = n_s // CORES
    width, rows_m = load_ref.shape
    rows_h, cols = act_ref.shape
    rank = rows_h * n_k
    pieces = rows_m // PIECE
    chunks = rows_m // chunk
    half = chunk // 2

    k, s = lax.axis_index("kmer"), lax.axis_index("samp")
    z, y = lax.div(k, n_y), lax.rem(k, n_y)
    x, core = lax.div(s, CORES), lax.rem(s, CORES)
    mate = x * CORES + (1 - core)

    def z_at(d):
        return lax.rem(z + d, n_z)

    def y_at(d):
        return lax.rem(y + d, n_y)

    def x_at(d):
        return lax.rem(x + d, n_x) * CORES + core

    def put(src, dst, send, recv, kk, ss):
        return pltpu.make_async_remote_copy(
            src_ref=src, dst_ref=dst, send_sem=send, recv_sem=recv,
            device_id={"kmer": kk, "samp": ss}, device_id_type=pl.DeviceIdType.MESH,
        )

    def block(start, size):
        return pl.ds(pl.multiple_of(start, size), size)

    def arrived(dst, sem):
        put(dst, dst, sem, sem, k, mate).wait_recv()

    sent = []

    def go(*args, when=None):
        copy = put(*args)
        sent.append((when, copy))
        if when is None:
            copy.start()
        else:
            pl.when(when)(copy.start)

    fetch = pltpu.make_async_copy(ab_hbm, ab, ab_sem)
    fetch.start()

    hbuf[block(k * rows_h, rows_h), :] = act_ref[...]
    wbuf[block(s * width, width), :] = load_ref[...]

    barrier = pltpu.get_barrier_semaphore()
    peers = [(lax.rem(k + d, n_k), s) for d in range(1, n_k)]
    peers += [(k, lax.rem(s + d, n_s)) for d in range(1, n_s)]
    for kk, ss in peers:
        pl.semaphore_signal(
            barrier, inc=1, device_id={"kmer": kk, "samp": ss}, device_id_type=pl.DeviceIdType.MESH
        )
    pl.semaphore_wait(barrier, len(peers))

    def hslot(kk):
        return hbuf.at[block(kk * rows_h, rows_h), :]

    def wslot(ss, j):
        return wbuf.at[block(ss * width, width), pl.ds(j * PIECE, PIECE)]

    def pass_h(zz, i, when):
        kk = zz * n_y + y
        slot = hslot(kk)
        up, down = jnp.minimum(z + 1, n_z - 1), jnp.maximum(z - 1, 0)
        if i >= 0:
            ok = z < n_z - 1
            go(slot, slot, hr_s.at[abs(i)], h_r.at[kk], up * n_y + y, s, when=ok if when is None else ok & when)
        if i <= 0:
            ok = z > 0
            go(slot, slot, hl_s.at[abs(i)], h_r.at[kk], down * n_y + y, s, when=ok if when is None else ok & when)
        for d in range(1, n_y):
            go(slot, slot, hy_s.at[n_z - 1 + i, d - 1], h_r.at[kk], z * n_y + y_at(d), s, when=when)

    pass_h(z, 0, None)
    for j in range(pieces):
        for d in range(1, n_x):
            go(wslot(s, j), wslot(s, j), wx_s.at[d - 1, j], w_r.at[s, j], k, x_at(d))
        go(wslot(s, j), wslot(s, j), wc_s.at[j], w_r.at[s, j], k, mate)

    def take_h(i):
        there = (z >= i) if i > 0 else (z - i <= n_z - 1)
        zz = jnp.clip(z - i, 0, n_z - 1)
        kk = zz * n_y + y

        @pl.when(there)
        def _():
            arrived(hslot(kk), h_r.at[kk])

        pass_h(zz, i, there)

    def take_w(j):
        for d in range(1, n_x):
            src = x_at(d)
            arrived(wslot(src, j), w_r.at[src, j])
            go(wslot(src, j), wslot(src, j), wf_s.at[d - 1, j], w_r.at[src, j], k, mate)

    for i in range(max(n_z - 1, pieces)):
        if i < n_z - 1:
            take_h(i + 1)
            take_h(-i - 1)
        if i < pieces:
            take_w(i)

    for j in range(pieces):
        for d in range(n_x):
            src = lax.rem(x + d, n_x) * CORES + (1 - core)
            arrived(wslot(src, j), w_r.at[src, j])
        for at in range(j * PIECE, (j + 1) * PIECE, chunk):
            whole = wbuf[:, at:at + chunk].T
            wfull[at:at + chunk, :] = whole
            high, low = halves(whole)
            w3[at:at + chunk, :] = jnp.concatenate([high, high, low], axis=1)

    for d in range(1, n_y):
        for i in range(n_z):
            src = i * n_y + y_at(d)
            arrived(hslot(src), h_r.at[src])

    high, low = halves(hbuf[...])
    h3[...] = jnp.concatenate([high, low, high], axis=0)
    turned = hbuf[...].T
    high, low = halves(turned)
    ht3[...] = jnp.concatenate([high, low, high], axis=0)
    tbuf[s] = jnp.broadcast_to(jnp.sum(turned, axis=0, keepdims=True), (8, rank))
    for d in range(1, n_s):
        go(tbuf.at[s], tbuf.at[s], t_s.at[d - 1], t_r.at[s], k, lax.rem(s + d, n_s))
    fetch.wait()

    def out_a(c):
        return put(
            nbuf.at[block(c * chunk + (1 - core) * half, half), :], recv_a.at[block(c * half, half), :],
            a_s.at[c], a_r.at[c], k, mate,
        )

    def out_x(c, d):
        rows = block(c * half, half)
        return put(sbuf.at[rows, :], recv_x.at[d - 1, rows, :], x_s.at[d - 1, c], x_r.at[d - 1, c], k, x_at(d))

    def out_u(c):
        rows = block(c * chunk + core * half, half)
        return put(ubuf.at[rows, :], ubuf.at[rows, :], u_s.at[c], u_r.at[c], k, mate)

    ahead = max(1, chunks // 2)

    def scale_rows(c):
        rows = block(c * half, half)
        total = sbuf[rows, :]
        for d in range(1, n_x):
            out_x(c, d).wait_recv()
            total = total + recv_x[d - 1, rows, :]
        mine = block(c * chunk + core * half, half)
        ubuf[mine, :] = wfull[mine, :] * total * tsum[0:1, :]
        out_u(c).start()

    def rows_step(c, carry):
        @pl.when(c < chunks)
        def _():
            rows = block(c * chunk, chunk)
            quotient = quotient_of(ab[rows, :], dot(w3[rows, :], h3[...]))
            high, low = halves(quotient)
            nbuf[rows, :] = dot(jnp.concatenate([high, high, low], axis=1), ht3[...])
            out_a(c).start()

        @pl.when(c == 1)
        def _():
            for d in range(1, n_s):
                src = lax.rem(s + d, n_s)
                arrived(tbuf.at[src], t_r.at[src])
            totals = tbuf[0]
            for i in range(1, n_s):
                totals = totals + tbuf[i]
            tsum[...] = 1.0 / totals

        @pl.when(c != 1)
        def _():
            b = jnp.maximum(c - 1, 0)
            out_a(b).wait_recv()
            rows = block(b * half, half)
            sbuf[rows, :] = nbuf[block(b * chunk + core * half, half), :] + recv_a[rows, :]
            for d in range(1, n_x):
                out_x(b, d).start()

        @pl.when(c > ahead)
        def _():
            scale_rows(c - 1 - ahead)

        return carry

    lax.fori_loop(0, chunks + 1, rows_step, 0)
    acc[...] = jnp.zeros_like(acc)
    csum[...] = jnp.zeros_like(csum)

    def cols_step(c, carry):
        @pl.when((c < chunks) & (c >= chunks - ahead))
        def _():
            scale_rows(c)

        @pl.when(c >= 1)
        def _():
            b = c - 1
            out_u(b).wait_recv()
            rows = block(b * chunk, chunk)
            updated = ubuf[rows, :]
            csum[...] += jnp.broadcast_to(jnp.sum(updated, axis=0, keepdims=True), csum.shape)
            high, low = halves(updated)
            rebuilt = dot(jnp.concatenate([high, high, low], axis=1), h3[...])
            q_high, q_low = halves(quotient_of(ab[rows, :], rebuilt))
            turned = updated.T
            uturn[:, rows] = turned
            high, low = halves(turned)
            acc[...] += dot(
                jnp.concatenate([high, high, low], axis=1), jnp.concatenate([q_high, q_low, q_high], axis=0)
            )

        return carry

    lax.fori_loop(0, chunks + 1, cols_step, 0)

    near = []
    for d in range(1, n_z // 2 + 1):
        near += [d] if d == n_z - d else [d, n_z - d]
    part = cols // PARTS
    steps = [(i, d, p) for i, d in enumerate(near[::-1] + [0]) for p in range(PARTS)]

    def part_of(p):
        return pl.ds(p * part, part)

    def send_y(i, d, p):
        for e in range(1, n_y):
            go(
                acc.at[block((z_at(d) * n_y + y_at(e)) * rows_h, rows_h), part_of(p)],
                recv_y.at[e - 1, i, :, part_of(p)],
                ry_s.at[e - 1, i, p], ry_r.at[e - 1, i, p], z * n_y + y_at(e), s,
            )

    for step in steps[:FLYING]:
        send_y(*step)
    cbuf[k] = csum[...]
    for d in range(1, n_k):
        go(cbuf.at[k], cbuf.at[k], c_s.at[d - 1], c_r.at[k], lax.rem(k + d, n_k), s)
    newload_ref[...] = uturn[block(s * width, width), :]

    for at, (i, d, p) in enumerate(steps):
        for e in range(1, n_y):
            arrived(recv_y.at[e - 1, i, :, part_of(p)], ry_r.at[e - 1, i, p])
        if at + FLYING < len(steps):
            send_y(*steps[at + FLYING])
        total = acc[block((z_at(d) * n_y + y) * rows_h, rows_h), part_of(p)]
        for e in range(1, n_y):
            total = total + recv_y[e - 1, i, :, part_of(p)]
        ybuf[i, :, part_of(p)] = total
        if d:
            go(
                ybuf.at[i, :, part_of(p)], recv_z.at[i, :, part_of(p)],
                rz_s.at[i, p], rz_r.at[i, p], z_at(d) * n_y + y, s,
            )

    for d in range(1, n_k):
        src = lax.rem(k + d, n_k)
        arrived(cbuf.at[src], c_r.at[src])
    sums = cbuf[0, 0:1, :]
    for i in range(1, n_k):
        sums = sums + cbuf[i, 0:1, :]
    uturn[:, 0:LANES] = jnp.broadcast_to(sums, (LANES, rank)).T
    scaled = act_ref[...] / uturn[block(k * rows_h, rows_h), 0:1]
    for p in range(PARTS):
        total = ybuf[n_z - 1, :, part_of(p)]
        for i in range(n_z - 1):
            arrived(recv_z.at[i, :, part_of(p)], rz_r.at[i, p])
            total = total + recv_z[i, :, part_of(p)]
        newact_ref[:, part_of(p)] = scaled[:, p * part:(p + 1) * part] * total

    for when, copy in sent:
        if when is None:
            copy.wait_send()
        else:
            pl.when(when)(copy.wait_send)

    def close(c, carry):
        out_a(c).wait_send()
        out_u(c).wait_send()
        for d in range(1, n_x):
            out_x(c, d).wait_send()
        return carry

    lax.fori_loop(0, chunks, close, 0)


def solution(mesh):
    n_k, n_s = mesh.shape["kmer"], mesh.shape["samp"]
    n_y = max(d for d in range(1, n_k + 1) if n_k % d == 0 and d * d <= n_k)
    n_z, n_x = n_k // n_y, n_s // CORES

    def per_device(abundance, loadings, activity):
        rows_m, width = loadings.shape
        rows_h, cols = activity.shape
        rank = rows_h * n_k
        chunk = 256
        chunks, pieces = rows_m // chunk, rows_m // PIECE
        vmem, dma = pltpu.VMEM, pltpu.SemaphoreType.DMA
        whole = pl.BlockSpec(memory_space=pltpu.VMEM)
        turned, updated = pl.pallas_call(
            functools.partial(kernel, (n_k, n_s, n_z, n_y, chunk)),
            out_shape=(
                jax.ShapeDtypeStruct((width, rows_m), F32),
                jax.ShapeDtypeStruct((rows_h, cols), F32),
            ),
            in_specs=[pl.BlockSpec(memory_space=pl.ANY), whole, whole],
            out_specs=(whole, whole),
            scratch_shapes=[
                vmem((rows_m, cols), F32),
                vmem((rank, rows_m), F32),
                vmem((rows_m, rank), F32),
                vmem((rows_m, 3 * rank), BF16),
                vmem((rank, cols), F32),
                vmem((3 * rank, cols), BF16),
                vmem((3 * cols, rank), BF16),
                vmem((n_s, 8, rank), F32),
                vmem((8, rank), F32),
                vmem((rows_m, rank), F32),
                vmem((rows_m // 2, rank), F32),
                vmem((rows_m // 2, rank), F32),
                vmem((n_x - 1, rows_m // 2, rank), F32),
                vmem((rows_m, rank), F32),
                vmem((rank, rows_m), F32),
                vmem((rank, cols), F32),
                vmem((n_k, 8, rank), F32),
                vmem((8, rank), F32),
                vmem((n_y - 1, n_z, rows_h, cols), F32),
                vmem((n_z, rows_h, cols), F32),
                vmem((n_z - 1, rows_h, cols), F32),
                dma,
                dma((n_z,)),
                dma((n_z,)),
                dma((2 * n_z - 1, n_y - 1)),
                dma((n_k,)),
                dma((n_x - 1, pieces)),
                dma((pieces,)),
                dma((n_x - 1, pieces)),
                dma((n_s, pieces)),
                dma((n_s - 1,)),
                dma((n_s,)),
                dma((chunks,)),
                dma((chunks,)),
                dma((n_x - 1, chunks)),
                dma((n_x - 1, chunks)),
                dma((chunks,)),
                dma((chunks,)),
                dma((n_k - 1,)),
                dma((n_k,)),
                dma((n_y - 1, n_z, PARTS)),
                dma((n_y - 1, n_z, PARTS)),
                dma((n_z - 1, PARTS)),
                dma((n_z - 1, PARTS)),
            ],
            compiler_params=pltpu.CompilerParams(
                collective_id=0, has_side_effects=True, vmem_limit_bytes=56 * 2**20
            ),
            cost_estimate=pl.CostEstimate(
                flops=24 * rows_m * cols * rank,
                bytes_accessed=4 * rows_m * cols,
                transcendentals=2 * rows_m * cols,
            ),
        )(abundance, loadings.T, activity)
        return turned.T, updated

    in_specs = (P("kmer", "samp"), P("kmer", "samp"), P("kmer", "samp"))
    out_specs = (P("kmer", "samp"), P("kmer", "samp"))
    return jax.shard_map(
        per_device, mesh=mesh, in_specs=in_specs, out_specs=out_specs, check_vma=False
    )
```

time: 81.3 us -> 75.9 us (0.934)
  local copies, waits for them, and re-layouts: 6.27 us -> 3.44 us
  Pallas kernels: 73.9 us -> 71.6 us
    pallas_call x1 -> x0, local copies, waits for them, and re-layouts: 2.34 us -> none  [per_device(): pl.pallas_call(functools.partial(kernel, (n_k, n_s, n_z, n_y, chunk)), ou...]
    pallas_call x1, Pallas kernels: 73.9 us -> 71.6 us  [per_device(): pl.pallas_call(functools.partial(kernel, (n_k, n_s, n_z, n_y, chunk)), ou...]
where the time goes in v2:
time: 75.9 us; the launch traced here: 75.7 us
  Pallas kernels  71.6 us (94%)
  local copies, waits for them, and re-layouts  3.44 us (5%)
    pallas_call x1, Pallas kernels, per_device(): pl.pallas_call(functools.partial(kernel, (n_k, n_s, n_z, n_y, chunk)), ou...  71.6 us
    unnamed x2, local copies, waits for them, and re-layouts  3.44 us

profile of v2, /device:TPU:0, one launch (start us, length us, event | category | flops | bytes accessed | tf_op | source)
XLA Modules:
  0.0 75.7 jit_solution(15184450912277885298)
XLA Ops:
  0.6 71.6 %shard_map.50 = (f32[64,2048]{1,0:T(8,128)}, f32[32,1024]{1,0:T(8,128)}) custom-call(f32[2048,1024]{1,0:T(8,128)} %ab_hbm.1, f32[64,2048]{1,0:T(8,128)} %bitcast.3, f32[32,1024]{1,0:T(8,128)} %act_ref.1), custom_call_target="tpu_custom_call" | custom-call | flops 12884901888 | bytes 8388608 | tf_op jit(solution)/shard_map/pallas_call | solution.py:345
  72.3 1.9 %copy.7 = f32[2048,64]{0,1:T(8,128)} copy(f32[2048,64]{0,1:T(8,128)} %bitcast.2) | data formatting | bytes 1048576
  74.1 1.6 %copy.8 = f32[32,1024]{1,0:T(8,128)} copy(f32[32,1024]{1,0:T(8,128)} %get-tuple-element.9) | data formatting | bytes 262144

commit v3 on v2

--- a/solution.py
+++ b/solution.py
@@ -31,7 +31,7 @@
 
 def kernel(
     sizes, ab_hbm, load_ref, act_ref, newload_ref, newact_ref,
-    ab, wbuf, wfull, w3, hbuf, h3, ht3, tbuf, tsum, nbuf, recv_a, sbuf, recv_x, ubuf, uturn, acc, cbuf, csum, recv_y, ybuf, recv_z,
+    ab, abt, wbuf, w3, hbuf, h3, ht3, tbuf, tsum, nbuf, recv_a, sbuf, recv_x, ubuf, acct, acc, cbuf, csum, column, recv_y, ybuf, recv_z,
     ab_sem, hr_s, hl_s, hy_s, h_r, wx_s, wc_s, wf_s, w_r, t_s, t_r, a_s, a_r, x_s, x_r, u_s, u_r, c_s, c_r,
     ry_s, ry_r, rz_s, rz_r,
 ):
@@ -42,7 +42,7 @@
     rank = rows_h * n_k
     pieces = rows_m // PIECE
     chunks = rows_m // chunk
-    half = chunk // 2
+    half = rank // 2
 
     k, s = lax.axis_index("kmer"), lax.axis_index("samp")
     z, y = lax.div(k, n_y), lax.rem(k, n_y)
@@ -137,22 +137,26 @@
             arrived(wslot(src, j), w_r.at[src, j])
             go(wslot(src, j), wslot(src, j), wf_s.at[d - 1, j], w_r.at[src, j], k, mate)
 
-    for i in range(max(n_z - 1, pieces)):
+    waits = max(n_z - 1, pieces)
+    turns = pl.cdiv(chunks, waits)
+    for i in range(waits):
         if i < n_z - 1:
             take_h(i + 1)
             take_h(-i - 1)
         if i < pieces:
             take_w(i)
+        if i == 0:
+            fetch.wait()
+        for at in range(i * turns * chunk, min((i + 1) * turns * chunk, rows_m), chunk):
+            abt[:, at:at + chunk] = ab[at:at + chunk, :].T
 
     for j in range(pieces):
         for d in range(n_x):
             src = lax.rem(x + d, n_x) * CORES + (1 - core)
             arrived(wslot(src, j), w_r.at[src, j])
-        for at in range(j * PIECE, (j + 1) * PIECE, chunk):
-            whole = wbuf[:, at:at + chunk].T
-            wfull[at:at + chunk, :] = whole
-            high, low = halves(whole)
-            w3[at:at + chunk, :] = jnp.concatenate([high, high, low], axis=1)
+        at = slice(j * PIECE, (j + 1) * PIECE)
+        high, low = halves(wbuf[:, at])
+        w3[:, at] = jnp.concatenate([high, low, high], axis=0)
 
     for d in range(1, n_y):
         for i in range(n_z):
@@ -160,48 +164,43 @@
             arrived(hslot(src), h_r.at[src])
 
     high, low = halves(hbuf[...])
-    h3[...] = jnp.concatenate([high, low, high], axis=0)
+    h3[...] = jnp.concatenate([high, high, low], axis=1)
     turned = hbuf[...].T
     high, low = halves(turned)
-    ht3[...] = jnp.concatenate([high, low, high], axis=0)
+    ht3[...] = jnp.concatenate([high, high, low], axis=1)
     tbuf[s] = jnp.broadcast_to(jnp.sum(turned, axis=0, keepdims=True), (8, rank))
     for d in range(1, n_s):
         go(tbuf.at[s], tbuf.at[s], t_s.at[d - 1], t_r.at[s], k, lax.rem(s + d, n_s))
-    fetch.wait()
+
+    mine = block(core * half, half)
 
     def out_a(c):
         return put(
-            nbuf.at[block(c * chunk + (1 - core) * half, half), :], recv_a.at[block(c * half, half), :],
-            a_s.at[c], a_r.at[c], k, mate,
+            nbuf.at[c, block((1 - core) * half, half), :], recv_a.at[c], a_s.at[c], a_r.at[c], k, mate
         )
 
     def out_x(c, d):
-        rows = block(c * half, half)
-        return put(sbuf.at[rows, :], recv_x.at[d - 1, rows, :], x_s.at[d - 1, c], x_r.at[d - 1, c], k, x_at(d))
+        return put(sbuf.at[c], recv_x.at[d - 1, c], x_s.at[d - 1, c], x_r.at[d - 1, c], k, x_at(d))
 
     def out_u(c):
-        rows = block(c * chunk + core * half, half)
-        return put(ubuf.at[rows, :], ubuf.at[rows, :], u_s.at[c], u_r.at[c], k, mate)
+        return put(ubuf.at[c, mine, :], ubuf.at[c, mine, :], u_s.at[c], u_r.at[c], k, mate)
 
     ahead = max(1, chunks // 2)
 
     def scale_rows(c):
-        rows = block(c * half, half)
-        total = sbuf[rows, :]
+        total = sbuf[c]
         for d in range(1, n_x):
             out_x(c, d).wait_recv()
-            total = total + recv_x[d - 1, rows, :]
-        mine = block(c * chunk + core * half, half)
-        ubuf[mine, :] = wfull[mine, :] * total * tsum[0:1, :]
+            total = total + recv_x[d - 1, c]
+        ubuf[c, mine, :] = wbuf[mine, block(c * chunk, chunk)] * total * tsum[mine, 0:1]
         out_u(c).start()
 
     def rows_step(c, carry):
         @pl.when(c < chunks)
         def _():
             rows = block(c * chunk, chunk)
-            quotient = quotient_of(ab[rows, :], dot(w3[rows, :], h3[...]))
-            high, low = halves(quotient)
-            nbuf[rows, :] = dot(jnp.concatenate([high, high, low], axis=1), ht3[...])
+            high, low = halves(quotient_of(abt[:, rows], dot(ht3[...], w3[:, rows])))
+            nbuf[c] = dot(h3[...], jnp.concatenate([high, low, high], axis=0))
             out_a(c).start()
 
         @pl.when(c == 1)
@@ -212,14 +211,13 @@
             totals = tbuf[0]
             for i in range(1, n_s):
                 totals = totals + tbuf[i]
-            tsum[...] = 1.0 / totals
+            tsum[...] = 1.0 / jnp.broadcast_to(totals[0:1, :], (LANES, rank)).T
 
         @pl.when(c != 1)
         def _():
             b = jnp.maximum(c - 1, 0)
             out_a(b).wait_recv()
-            rows = block(b * half, half)
-            sbuf[rows, :] = nbuf[block(b * chunk + core * half, half), :] + recv_a[rows, :]
+            sbuf[b] = nbuf[b, mine, :] + recv_a[b]
             for d in range(1, n_x):
                 out_x(b, d).start()
 
@@ -230,7 +228,7 @@
         return carry
 
     lax.fori_loop(0, chunks + 1, rows_step, 0)
-    acc[...] = jnp.zeros_like(acc)
+    acct[...] = jnp.zeros_like(acct)
     csum[...] = jnp.zeros_like(csum)
 
     def cols_step(c, carry):
@@ -242,22 +240,21 @@
         def _():
             b = c - 1
             out_u(b).wait_recv()
-            rows = block(b * chunk, chunk)
-            updated = ubuf[rows, :]
-            csum[...] += jnp.broadcast_to(jnp.sum(updated, axis=0, keepdims=True), csum.shape)
+            updated = ubuf[b]
             high, low = halves(updated)
-            rebuilt = dot(jnp.concatenate([high, high, low], axis=1), h3[...])
-            q_high, q_low = halves(quotient_of(ab[rows, :], rebuilt))
+            rebuilt = dot(ht3[...], jnp.concatenate([high, low, high], axis=0))
+            q_high, q_low = halves(quotient_of(abt[:, block(b * chunk, chunk)], rebuilt))
             turned = updated.T
-            uturn[:, rows] = turned
+            csum[...] += jnp.broadcast_to(jnp.sum(turned, axis=0, keepdims=True), csum.shape)
             high, low = halves(turned)
-            acc[...] += dot(
-                jnp.concatenate([high, high, low], axis=1), jnp.concatenate([q_high, q_low, q_high], axis=0)
+            acct[...] += dot(
+                jnp.concatenate([q_high, q_high, q_low], axis=1), jnp.concatenate([high, low, high], axis=0)
             )
 
         return carry
 
     lax.fori_loop(0, chunks + 1, cols_step, 0)
+    acc[...] = acct[...].T
 
     near = []
     for d in range(1, n_z // 2 + 1):
@@ -281,7 +278,8 @@
     cbuf[k] = csum[...]
     for d in range(1, n_k):
         go(cbuf.at[k], cbuf.at[k], c_s.at[d - 1], c_r.at[k], lax.rem(k + d, n_k), s)
-    newload_ref[...] = uturn[block(s * width, width), :]
+    for c in range(chunks):
+        newload_ref[:, c * chunk:(c + 1) * chunk] = ubuf[c, block(s * width, width), :]
 
     for at, (i, d, p) in enumerate(steps):
         for e in range(1, n_y):
@@ -304,8 +302,8 @@
     sums = cbuf[0, 0:1, :]
     for i in range(1, n_k):
         sums = sums + cbuf[i, 0:1, :]
-    uturn[:, 0:LANES] = jnp.broadcast_to(sums, (LANES, rank)).T
-    scaled = act_ref[...] / uturn[block(k * rows_h, rows_h), 0:1]
+    column[...] = jnp.broadcast_to(sums, (LANES, rank)).T
+    scaled = act_ref[...] / column[block(k * rows_h, rows_h), 0:1]
     for p in range(PARTS):
         total = ybuf[n_z - 1, :, part_of(p)]
         for i in range(n_z - 1):
@@ -327,6 +325,17 @@
         return carry
 
     lax.fori_loop(0, chunks, close, 0)
+
+
+def hand_over(load_in, act_in, load_out, act_out, sems):
+    copies = [
+        pltpu.make_async_copy(load_in, load_out, sems.at[0]),
+        pltpu.make_async_copy(act_in, act_out, sems.at[1]),
+    ]
+    for copy in copies:
+        copy.start()
+    for copy in copies:
+        copy.wait()
 
 
 def solution(mesh):
@@ -352,23 +361,24 @@
             out_specs=(whole, whole),
             scratch_shapes=[
                 vmem((rows_m, cols), F32),
+                vmem((cols, rows_m), F32),
                 vmem((rank, rows_m), F32),
-                vmem((rows_m, rank), F32),
-                vmem((rows_m, 3 * rank), BF16),
+                vmem((3 * rank, rows_m), BF16),
                 vmem((rank, cols), F32),
-                vmem((3 * rank, cols), BF16),
-                vmem((3 * cols, rank), BF16),
+                vmem((rank, 3 * cols), BF16),
+                vmem((cols, 3 * rank), BF16),
                 vmem((n_s, 8, rank), F32),
-                vmem((8, rank), F32),
-                vmem((rows_m, rank), F32),
-                vmem((rows_m // 2, rank), F32),
-                vmem((rows_m // 2, rank), F32),
-                vmem((n_x - 1, rows_m // 2, rank), F32),
-                vmem((rows_m, rank), F32),
-                vmem((rank, rows_m), F32),
+                vmem((rank, LANES), F32),
+                vmem((chunks, rank, chunk), F32),
+                vmem((chunks, rank // 2, chunk), F32),
+                vmem((chunks, rank // 2, chunk), F32),
+                vmem((n_x - 1, chunks, rank // 2, chunk), F32),
+                vmem((chunks, rank, chunk), F32),
+                vmem((cols, rank), F32),
                 vmem((rank, cols), F32),
                 vmem((n_k, 8, rank), F32),
                 vmem((8, rank), F32),
+                vmem((rank, LANES), F32),
                 vmem((n_y - 1, n_z, rows_h, cols), F32),
                 vmem((n_z, rows_h, cols), F32),
                 vmem((n_z - 1, rows_h, cols), F32),
@@ -405,6 +415,18 @@
                 transcendentals=2 * rows_m * cols,
             ),
         )(abundance, loadings.T, activity)
+        anywhere = pl.BlockSpec(memory_space=pl.ANY)
+        turned, updated = pl.pallas_call(
+            hand_over,
+            out_shape=(
+                jax.ShapeDtypeStruct((width, rows_m), F32),
+                jax.ShapeDtypeStruct((rows_h, cols), F32),
+            ),
+            in_specs=[anywhere, anywhere],
+            out_specs=(anywhere, anywhere),
+            scratch_shapes=[dma((2,))],
+            compiler_params=pltpu.CompilerParams(vmem_limit_bytes=56 * 2**20),
+        )(turned, updated)
         return turned.T, updated
 
     in_specs = (P("kmer", "samp"), P("kmer", "samp"), P("kmer", "samp"))

time: 75.9 us -> 95 us (1.25)
  Pallas kernels: 71.6 us -> 94.2 us
  local copies, waits for them, and re-layouts: 3.44 us -> 0 us
    pallas_call x0 -> x1, Pallas kernels: none -> 21 us  [per_device(): pl.pallas_call(hand_over, out_shape=(jax.ShapeDtypeStruct((width, rows_m)...]
    unnamed x2 -> x0, local copies, waits for them, and re-layouts: 3.44 us -> none
    pallas_call x1, Pallas kernels: 71.6 us -> 73.2 us  [per_device(): pl.pallas_call(functools.partial(kernel, (n_k, n_s, n_z, n_y, chunk)), ou...]
where the time goes in v3:
time: 95 us; the launch traced here: 94.8 us
  Pallas kernels  94.2 us (99%)
    pallas_call x1, Pallas kernels, per_device(): pl.pallas_call(functools.partial(kernel, (n_k, n_s, n_z, n_y, chunk)), ou...  73.2 us
    pallas_call x1, Pallas kernels, per_device(): pl.pallas_call(hand_over, out_shape=(jax.ShapeDtypeStruct((width, rows_m)...  21 us

profile of v3, /device:TPU:0, one launch (start us, length us, event | category | flops | bytes accessed | tf_op | source)
XLA Modules:
  0.0 94.8 jit_solution(1602179137786414654)
XLA Ops:
  0.6 73.2 %shard_map.50 = (f32[64,2048]{1,0:T(8,128)}, f32[32,1024]{1,0:T(8,128)}) custom-call(f32[2048,1024]{1,0:T(8,128)} %ab_hbm.1, f32[64,2048]{1,0:T(8,128)} %bitcast.2, f32[32,1024]{1,0:T(8,128)} %act_ref.1), custom_call_target="tpu_custom_call" | custom-call | flops 12884901888 | bytes 8388608 | tf_op jit(solution)/shard_map/pallas_call | solution.py:354
  73.9 21.0 %shard_map.51 = (f32[64,2048]{1,0:T(8,128)}, f32[32,1024]{1,0:T(8,128)}) custom-call(f32[64,2048]{1,0:T(8,128)} %get-tuple-element.6.load_in, f32[32,1024]{1,0:T(8,128)} %get-tuple-element.7.act_in), custom_call_target="tpu_custom_call" | custom-call | tf_op jit(solution)/shard_map/pallas_call | solution.py:419

commit v4 on v3

--- a/solution.py
+++ b/solution.py
@@ -12,6 +12,7 @@
 PIECE = 512
 PARTS = 2
 FLYING = 3
+HOPS = 2
 CORES = 2
 
 
@@ -80,8 +81,12 @@
         else:
             pl.when(when)(copy.start)
 
-    fetch = pltpu.make_async_copy(ab_hbm, ab, ab_sem)
-    fetch.start()
+    def fetch(c):
+        rows = pl.ds(c * chunk, chunk)
+        return pltpu.make_async_copy(ab_hbm.at[rows, :], ab.at[rows, :], ab_sem.at[c])
+
+    for c in range(chunks):
+        fetch(c).start()
 
     hbuf[block(k * rows_h, rows_h), :] = act_ref[...]
     wbuf[block(s * width, width), :] = load_ref[...]
@@ -95,41 +100,44 @@
         )
     pl.semaphore_wait(barrier, len(peers))
 
-    def hslot(kk):
-        return hbuf.at[block(kk * rows_h, rows_h), :]
+    part_h = cols // HOPS
+
+    def hslot(kk, p):
+        return hbuf.at[block(kk * rows_h, rows_h), pl.ds(p * part_h, part_h)]
 
     def wslot(ss, j):
         return wbuf.at[block(ss * width, width), pl.ds(j * PIECE, PIECE)]
 
-    def pass_h(zz, i, when):
+    def pass_h(zz, i, p, when):
         kk = zz * n_y + y
-        slot = hslot(kk)
+        slot, recv = hslot(kk, p), h_r.at[kk, p]
         up, down = jnp.minimum(z + 1, n_z - 1), jnp.maximum(z - 1, 0)
         if i >= 0:
             ok = z < n_z - 1
-            go(slot, slot, hr_s.at[abs(i)], h_r.at[kk], up * n_y + y, s, when=ok if when is None else ok & when)
+            go(slot, slot, hr_s.at[abs(i), p], recv, up * n_y + y, s, when=ok if when is None else ok & when)
         if i <= 0:
             ok = z > 0
-            go(slot, slot, hl_s.at[abs(i)], h_r.at[kk], down * n_y + y, s, when=ok if when is None else ok & when)
+            go(slot, slot, hl_s.at[abs(i), p], recv, down * n_y + y, s, when=ok if when is None else ok & when)
         for d in range(1, n_y):
-            go(slot, slot, hy_s.at[n_z - 1 + i, d - 1], h_r.at[kk], z * n_y + y_at(d), s, when=when)
-
-    pass_h(z, 0, None)
+            go(slot, slot, hy_s.at[n_z - 1 + i, d - 1, p], recv, z * n_y + y_at(d), s, when=when)
+
+    for p in range(HOPS):
+        pass_h(z, 0, p, None)
     for j in range(pieces):
         for d in range(1, n_x):
             go(wslot(s, j), wslot(s, j), wx_s.at[d - 1, j], w_r.at[s, j], k, x_at(d))
         go(wslot(s, j), wslot(s, j), wc_s.at[j], w_r.at[s, j], k, mate)
 
-    def take_h(i):
+    def take_h(i, p):
         there = (z >= i) if i > 0 else (z - i <= n_z - 1)
         zz = jnp.clip(z - i, 0, n_z - 1)
         kk = zz * n_y + y
 
         @pl.when(there)
         def _():
-            arrived(hslot(kk), h_r.at[kk])
-
-        pass_h(zz, i, there)
+            arrived(hslot(kk, p), h_r.at[kk, p])
+
+        pass_h(zz, i, p, there)
 
     def take_w(j):
         for d in range(1, n_x):
@@ -141,14 +149,15 @@
     turns = pl.cdiv(chunks, waits)
     for i in range(waits):
         if i < n_z - 1:
-            take_h(i + 1)
-            take_h(-i - 1)
+            for p in range(HOPS):
+                take_h(i + 1, p)
+                take_h(-i - 1, p)
         if i < pieces:
             take_w(i)
-        if i == 0:
-            fetch.wait()
-        for at in range(i * turns * chunk, min((i + 1) * turns * chunk, rows_m), chunk):
-            abt[:, at:at + chunk] = ab[at:at + chunk, :].T
+        for c in range(i * turns, min((i + 1) * turns, chunks)):
+            fetch(c).wait()
+            at = slice(c * chunk, (c + 1) * chunk)
+            abt[:, at] = ab[at, :].T
 
     for j in range(pieces):
         for d in range(n_x):
@@ -158,17 +167,21 @@
         high, low = halves(wbuf[:, at])
         w3[:, at] = jnp.concatenate([high, low, high], axis=0)
 
-    for d in range(1, n_y):
-        for i in range(n_z):
-            src = i * n_y + y_at(d)
-            arrived(hslot(src), h_r.at[src])
-
-    high, low = halves(hbuf[...])
-    h3[...] = jnp.concatenate([high, high, low], axis=1)
-    turned = hbuf[...].T
-    high, low = halves(turned)
-    ht3[...] = jnp.concatenate([high, high, low], axis=1)
-    tbuf[s] = jnp.broadcast_to(jnp.sum(turned, axis=0, keepdims=True), (8, rank))
+    row_totals = jnp.zeros((1, rank), F32)
+    for p in range(HOPS):
+        for d in range(1, n_y):
+            for i in range(n_z):
+                src = i * n_y + y_at(d)
+                arrived(hslot(src, p), h_r.at[src, p])
+        at = slice(p * part_h, (p + 1) * part_h)
+        high, low = halves(hbuf[:, at])
+        h3[:, at], h3[:, cols + p * part_h:cols + (p + 1) * part_h] = high, high
+        h3[:, 2 * cols + p * part_h:2 * cols + (p + 1) * part_h] = low
+        turned = hbuf[:, at].T
+        high, low = halves(turned)
+        ht3[at, :] = jnp.concatenate([high, high, low], axis=1)
+        row_totals = row_totals + jnp.sum(turned, axis=0, keepdims=True)
+    tbuf[s] = jnp.broadcast_to(row_totals, (8, rank))
     for d in range(1, n_s):
         go(tbuf.at[s], tbuf.at[s], t_s.at[d - 1], t_r.at[s], k, lax.rem(s + d, n_s))
 
@@ -327,15 +340,9 @@
     lax.fori_loop(0, chunks, close, 0)
 
 
-def hand_over(load_in, act_in, load_out, act_out, sems):
-    copies = [
-        pltpu.make_async_copy(load_in, load_out, sems.at[0]),
-        pltpu.make_async_copy(act_in, act_out, sems.at[1]),
-    ]
-    for copy in copies:
-        copy.start()
-    for copy in copies:
-        copy.wait()
+def hand_over(load_in, act_in, load_out, act_out):
+    load_out[...] = load_in[...]
+    act_out[...] = act_in[...]
 
 
 def solution(mesh):
@@ -382,11 +389,11 @@
                 vmem((n_y - 1, n_z, rows_h, cols), F32),
                 vmem((n_z, rows_h, cols), F32),
                 vmem((n_z - 1, rows_h, cols), F32),
-                dma,
-                dma((n_z,)),
-                dma((n_z,)),
-                dma((2 * n_z - 1, n_y - 1)),
-                dma((n_k,)),
+                dma((chunks,)),
+                dma((n_z, HOPS)),
+                dma((n_z, HOPS)),
+                dma((2 * n_z - 1, n_y - 1, HOPS)),
+                dma((n_k, HOPS)),
                 dma((n_x - 1, pieces)),
                 dma((pieces,)),
                 dma((n_x - 1, pieces)),
@@ -415,17 +422,14 @@
                 transcendentals=2 * rows_m * cols,
             ),
         )(abundance, loadings.T, activity)
-        anywhere = pl.BlockSpec(memory_space=pl.ANY)
         turned, updated = pl.pallas_call(
             hand_over,
             out_shape=(
                 jax.ShapeDtypeStruct((width, rows_m), F32),
                 jax.ShapeDtypeStruct((rows_h, cols), F32),
             ),
-            in_specs=[anywhere, anywhere],
-            out_specs=(anywhere, anywhere),
-            scratch_shapes=[dma((2,))],
-            compiler_params=pltpu.CompilerParams(vmem_limit_bytes=56 * 2**20),
+            in_specs=[whole, whole],
+            out_specs=(whole, whole),
         )(turned, updated)
         return turned.T, updated
 

time: 95 us -> 74.5 us (0.78)
  Pallas kernels: 94.2 us -> 73.7 us
    pallas_call x1, Pallas kernels: 21 us -> 1.93 us  [per_device(): pl.pallas_call(hand_over, out_shape=(jax.ShapeDtypeStruct((width, rows_m)...]
    pallas_call x1, Pallas kernels: 73.2 us -> 71.7 us  [per_device(): pl.pallas_call(functools.partial(kernel, (n_k, n_s, n_z, n_y, chunk)), ou...]
where the time goes in v4:
time: 74.5 us; the launch traced here: 74.3 us
  Pallas kernels  73.7 us (99%)
    pallas_call x1, Pallas kernels, per_device(): pl.pallas_call(functools.partial(kernel, (n_k, n_s, n_z, n_y, chunk)), ou...  71.7 us
    pallas_call x1, Pallas kernels, per_device(): pl.pallas_call(hand_over, out_shape=(jax.ShapeDtypeStruct((width, rows_m)...  1.93 us

profile of v4, /device:TPU:0, one launch (start us, length us, event | category | flops | bytes accessed | tf_op | source)
XLA Modules:
  0.0 74.3 jit_solution(956913013455094088)
XLA Ops:
  0.6 71.7 %shard_map.50 = (f32[64,2048]{1,0:T(8,128)}, f32[32,1024]{1,0:T(8,128)}) custom-call(f32[2048,1024]{1,0:T(8,128)} %ab_hbm.1, f32[64,2048]{1,0:T(8,128)} %bitcast.2, f32[32,1024]{1,0:T(8,128)} %act_ref.1), custom_call_target="tpu_custom_call" | custom-call | flops 12884901888 | bytes 8388608 | tf_op jit(solution)/shard_map/pallas_call | solution.py:361
  72.4 1.9 %shard_map.51 = (f32[64,2048]{1,0:T(8,128)}, f32[32,1024]{1,0:T(8,128)}) custom-call(f32[64,2048]{1,0:T(8,128)} %get-tuple-element.6.load_in, f32[32,1024]{1,0:T(8,128)} %get-tuple-element.7.act_in), custom_call_target="tpu_custom_call" | custom-call | tf_op jit(solution)/shard_map/pallas_call | solution.py:425

commit v5 on v4

--- a/solution.py
+++ b/solution.py
@@ -354,7 +354,7 @@
         rows_m, width = loadings.shape
         rows_h, cols = activity.shape
         rank = rows_h * n_k
-        chunk = 256
+        chunk = 512
         chunks, pieces = rows_m // chunk, rows_m // PIECE
         vmem, dma = pltpu.VMEM, pltpu.SemaphoreType.DMA
         whole = pl.BlockSpec(memory_space=pltpu.VMEM)

time: 74.5 us -> 76.5 us (1.027)
  Pallas kernels: 73.7 us -> 75.7 us
    pallas_call x1, Pallas kernels: 71.7 us -> 73.8 us  [per_device(): pl.pallas_call(functools.partial(kernel, (n_k, n_s, n_z, n_y, chunk)), ou...]
where the time goes in v5:
time: 76.5 us; the launch traced here: 76.4 us
  Pallas kernels  75.7 us (99%)
    pallas_call x1, Pallas kernels, per_device(): pl.pallas_call(functools.partial(kernel, (n_k, n_s, n_z, n_y, chunk)), ou...  73.8 us
    pallas_call x1, Pallas kernels, per_device(): pl.pallas_call(hand_over, out_shape=(jax.ShapeDtypeStruct((width, rows_m)...  1.93 us

profile of v5, /device:TPU:0, one launch (start us, length us, event | category | flops | bytes accessed | tf_op | source)
XLA Modules:
  0.0 76.4 jit_solution(15518589098764139563)
XLA Ops:
  0.6 73.8 %shard_map.50 = (f32[64,2048]{1,0:T(8,128)}, f32[32,1024]{1,0:T(8,128)}) custom-call(f32[2048,1024]{1,0:T(8,128)} %ab_hbm.1, f32[64,2048]{1,0:T(8,128)} %bitcast.2, f32[32,1024]{1,0:T(8,128)} %act_ref.1), custom_call_target="tpu_custom_call" | custom-call | flops 12884901888 | bytes 8388608 | tf_op jit(solution)/shard_map/pallas_call | solution.py:361
  74.4 1.9 %shard_map.51 = (f32[64,2048]{1,0:T(8,128)}, f32[32,1024]{1,0:T(8,128)}) custom-call(f32[64,2048]{1,0:T(8,128)} %get-tuple-element.6.load_in, f32[32,1024]{1,0:T(8,128)} %get-tuple-element.7.act_in), custom_call_target="tpu_custom_call" | custom-call | tf_op jit(solution)/shard_map/pallas_call | solution.py:425

commit v6 on v4

--- a/solution.py
+++ b/solution.py
@@ -13,6 +13,7 @@
 PARTS = 2
 FLYING = 3
 HOPS = 2
+TILES = 2
 CORES = 2
 
 
@@ -175,8 +176,7 @@
                 arrived(hslot(src, p), h_r.at[src, p])
         at = slice(p * part_h, (p + 1) * part_h)
         high, low = halves(hbuf[:, at])
-        h3[:, at], h3[:, cols + p * part_h:cols + (p + 1) * part_h] = high, high
-        h3[:, 2 * cols + p * part_h:2 * cols + (p + 1) * part_h] = low
+        h3[:, at] = jnp.concatenate([high, low], axis=0)
         turned = hbuf[:, at].T
         high, low = halves(turned)
         ht3[at, :] = jnp.concatenate([high, high, low], axis=1)
@@ -199,6 +199,8 @@
         return put(ubuf.at[c, mine, :], ubuf.at[c, mine, :], u_s.at[c], u_r.at[c], k, mate)
 
     ahead = max(1, chunks // 2)
+    tile = cols // TILES
+    tiles = [slice(i * tile, (i + 1) * tile) for i in range(TILES)]
 
     def scale_rows(c):
         total = sbuf[c]
@@ -212,8 +214,12 @@
         @pl.when(c < chunks)
         def _():
             rows = block(c * chunk, chunk)
-            high, low = halves(quotient_of(abt[:, rows], dot(ht3[...], w3[:, rows])))
-            nbuf[c] = dot(h3[...], jnp.concatenate([high, low, high], axis=0))
+            numer = jnp.zeros((rank, chunk), F32)
+            for at in tiles:
+                high, low = halves(quotient_of(abt[at, rows], dot(ht3[at, :], w3[:, rows])))
+                both = dot(h3[:, at], high)
+                numer = numer + both[:rank] + both[rank:] + dot(h3[:rank, at], low)
+            nbuf[c] = numer
             out_a(c).start()
 
         @pl.when(c == 1)
@@ -255,14 +261,15 @@
             out_u(b).wait_recv()
             updated = ubuf[b]
             high, low = halves(updated)
-            rebuilt = dot(ht3[...], jnp.concatenate([high, low, high], axis=0))
-            q_high, q_low = halves(quotient_of(abt[:, block(b * chunk, chunk)], rebuilt))
+            right = jnp.concatenate([high, low, high], axis=0)
             turned = updated.T
             csum[...] += jnp.broadcast_to(jnp.sum(turned, axis=0, keepdims=True), csum.shape)
             high, low = halves(turned)
-            acct[...] += dot(
-                jnp.concatenate([q_high, q_high, q_low], axis=1), jnp.concatenate([high, low, high], axis=0)
-            )
+            left = jnp.concatenate([high, low, high], axis=0)
+            for at in tiles:
+                rebuilt = dot(ht3[at, :], right)
+                q_high, q_low = halves(quotient_of(abt[at, block(b * chunk, chunk)], rebuilt))
+                acct[at, :] += dot(jnp.concatenate([q_high, q_high, q_low], axis=1), left)
 
         return carry
 
@@ -372,7 +379,7 @@
                 vmem((rank, rows_m), F32),
                 vmem((3 * rank, rows_m), BF16),
                 vmem((rank, cols), F32),
-                vmem((rank, 3 * cols), BF16),
+                vmem((2 * rank, cols), BF16),
                 vmem((cols, 3 * rank), BF16),
                 vmem((n_s, 8, rank), F32),
                 vmem((rank, LANES), F32),

time: 74.5 us -> 73.2 us (0.983)
  Pallas kernels: 73.7 us -> 72.4 us
    pallas_call x1, Pallas kernels: 71.7 us -> 70.5 us  [per_device(): pl.pallas_call(functools.partial(kernel, (n_k, n_s, n_z, n_y, chunk)), ou...]
where the time goes in v6:
time: 73.2 us; the launch traced here: 73 us
  Pallas kernels  72.4 us (99%)
    pallas_call x1, Pallas kernels, per_device(): pl.pallas_call(functools.partial(kernel, (n_k, n_s, n_z, n_y, chunk)), ou...  70.5 us
    pallas_call x1, Pallas kernels, per_device(): pl.pallas_call(hand_over, out_shape=(jax.ShapeDtypeStruct((width, rows_m)...  1.93 us

profile of v6, /device:TPU:0, one launch (start us, length us, event | category | flops | bytes accessed | tf_op | source)
XLA Modules:
  0.0 73.0 jit_solution(13077460331640621350)
XLA Ops:
  0.6 70.5 %shard_map.50 = (f32[64,2048]{1,0:T(8,128)}, f32[32,1024]{1,0:T(8,128)}) custom-call(f32[2048,1024]{1,0:T(8,128)} %ab_hbm.1, f32[64,2048]{1,0:T(8,128)} %bitcast.2, f32[32,1024]{1,0:T(8,128)} %act_ref.1), custom_call_target="tpu_custom_call" | custom-call | flops 12884901888 | bytes 8388608 | tf_op jit(solution)/shard_map/pallas_call | solution.py:368
  71.1 1.9 %shard_map.51 = (f32[64,2048]{1,0:T(8,128)}, f32[32,1024]{1,0:T(8,128)}) custom-call(f32[64,2048]{1,0:T(8,128)} %get-tuple-element.6.load_in, f32[32,1024]{1,0:T(8,128)} %get-tuple-element.7.act_in), custom_call_target="tpu_custom_call" | custom-call | tf_op jit(solution)/shard_map/pallas_call | solution.py:432

commit v7 on v6

--- a/solution.py
+++ b/solution.py
@@ -13,7 +13,7 @@
 PARTS = 2
 FLYING = 3
 HOPS = 2
-TILES = 2
+TILES = 4
 CORES = 2
 
 

time: 73.2 us -> 72.6 us (level)
  no operation moved by 1% of the time
where the time goes in v7:
time: 72.6 us; the launch traced here: 72.4 us
  Pallas kernels  71.8 us (99%)
    pallas_call x1, Pallas kernels, per_device(): pl.pallas_call(functools.partial(kernel, (n_k, n_s, n_z, n_y, chunk)), ou...  69.9 us
    pallas_call x1, Pallas kernels, per_device(): pl.pallas_call(hand_over, out_shape=(jax.ShapeDtypeStruct((width, rows_m)...  1.93 us

profile of v7, /device:TPU:0, one launch (start us, length us, event | category | flops | bytes accessed | tf_op | source)
XLA Modules:
  0.0 72.4 jit_solution(7144606226543357139)
XLA Ops:
  0.6 69.9 %shard_map.50 = (f32[64,2048]{1,0:T(8,128)}, f32[32,1024]{1,0:T(8,128)}) custom-call(f32[2048,1024]{1,0:T(8,128)} %ab_hbm.1, f32[64,2048]{1,0:T(8,128)} %bitcast.2, f32[32,1024]{1,0:T(8,128)} %act_ref.1), custom_call_target="tpu_custom_call" | custom-call | flops 12884901888 | bytes 8388608 | tf_op jit(solution)/shard_map/pallas_call | solution.py:368
  70.5 1.9 %shard_map.51 = (f32[64,2048]{1,0:T(8,128)}, f32[32,1024]{1,0:T(8,128)}) custom-call(f32[64,2048]{1,0:T(8,128)} %get-tuple-element.6.load_in, f32[32,1024]{1,0:T(8,128)} %get-tuple-element.7.act_in), custom_call_target="tpu_custom_call" | custom-call | tf_op jit(solution)/shard_map/pallas_call | solution.py:432
